TPU v7x, 32 devices: a whole 2x2x4 slice. The times are simulated.
32 devices in a mesh: dom: 2 (over y), dp: 2 (over x), expert: 8 (over z, core).
Axes of the slice: x: 2, y: 2, z: 4, core: 2. Of those that a mesh axis runs over, the one named last changes fastest.
Arguments:
- hidden: bfloat16 [4, 8, 16, 66, 1280], P(('dom', 'dp'), None, 'expert'), parts along dimension 0, may hold values from -6 to 6
- expert_choice_index: int32 [4096, 8], P(('dom', 'dp', 'expert')), parts along dimension 0, may hold values from 0 to 15, all different within a row; in each aligned block of 128 rows (0 to 127, 128 to 255, ...) at most 66 rows name the same one
- gates: float32 [4096, 8], P(('dom', 'dp', 'expert')), parts along dimension 0, may hold values from 0.02 to 0.3
- down_adapter_hidden: bfloat16 [16, 32, 1280], P('expert', None, 'dp'), may hold values from -0.15625 to 0.15625
- hidden_tangent: bfloat16 [32, 32, 1280], P(('dom', 'expert'), None, 'dp'), parts along dimension 0, may hold values from -0.15625 to 0.15625
- down_adapter_output: bfloat16 [16, 32, 3584], P('expert'), may hold values from -1 to 1
- output_tangent_factor: bfloat16 [32, 32, 3584], P(('dom', 'expert')), parts along dimension 0, may hold values from -1 to 1
Outputs:
- grad_a: float32 [32, 32, 1280], P(('dom', 'expert'), None, 'dp'), parts along dimension 0
- grad_b: float32 [32, 32, 3584], P(('dom', 'expert'), None, 'dp'), parts along dimension 0
There are 2 independent parts, one for each index of `dom`. A program takes and returns all parts, laid end to end along the dimension named above; an argument that names none is the same for every part. Nothing has to cross between parts.
Inputs may be any that keep to these rules, and one draw needn't show every extreme that they name: `expert_choice_index`: each row names 8 different experts. In each aligned block of 128 rows (the rows of one device) no expert is named by more than 66 rows, and in every draw some block names some expert exactly 66 times.
All inputs are finite; a program needn't handle non-finite values.
Results may differ from a plain program's by a relative error of at most 0.0035.
Values may be sent and summed in bfloat16 or wider, within the bound.
A program may use at most 128 MiB of HBM per device.

v0:
```python
import jax
import jax.numpy as jnp
from jax import lax
from jax.sharding import PartitionSpec as P


def on_device(
    hidden,
    expert_choice_index,
    gates,
    down_adapter_hidden,
    hidden_tangent,
    down_adapter_output,
    output_tangent_factor,
):
    cached = hidden[0]
    groups, exp_dev, slots_per, hidden_width = cached.shape
    tok_dev, choose = expert_choice_index.shape
    adapter_rank_size = down_adapter_output.shape[1]
    layer_width = down_adapter_output.shape[2]
    shards = lax.axis_size("dp")
    experts = groups * exp_dev
    adapter_pieces = jnp.concatenate([down_adapter_hidden, hidden_tangent], axis=1)
    adapter_set = lax.all_gather(adapter_pieces, "dp", axis=2, tiled=True)
    projected_result = jnp.einsum(
        "secf,erf->secr", cached, adapter_set, preferred_element_type=jnp.float32
    ).astype(jnp.bfloat16)
    projected_hidden = projected_result[..., :adapter_rank_size]
    stacked_factors = jnp.concatenate([output_tangent_factor, down_adapter_output], axis=1)
    tangent_row_block = jnp.einsum(
        "pibx,ixm->pibm", projected_result, stacked_factors, preferred_element_type=jnp.float32
    ).astype(jnp.bfloat16)
    returned = lax.all_to_all(tangent_row_block, "expert", split_axis=0, concat_axis=0, tiled=True)
    flat_ids = expert_choice_index.reshape(-1)
    labels = jnp.arange(experts, dtype=jnp.int32)
    matches = (flat_ids[:, None] == labels[None, :]).astype(jnp.int32)
    before = jnp.cumsum(matches, axis=0) - matches
    slot_index = jnp.sum(before * matches, axis=1)
    positions = flat_ids * slots_per + slot_index
    returned_flat = returned.reshape(experts * slots_per, layer_width)
    picked = jnp.take(returned_flat, positions, axis=0).reshape(tok_dev, choose, layer_width)
    output_tangent = jnp.sum(gates[:, :, None] * picked.astype(jnp.float32), axis=1)
    total_slots = experts * slots_per
    token_of_pair = jnp.arange(tok_dev * choose, dtype=jnp.int32) // choose
    slot_token = jnp.zeros((total_slots,), jnp.int32).at[positions].set(token_of_pair)
    slot_gate = jnp.zeros((total_slots,), jnp.float32).at[positions].set(gates.reshape(-1))
    cot_out = (slot_gate[:, None] * jnp.take(output_tangent, slot_token, axis=0)).astype(
        jnp.bfloat16
    )
    cot_out = cot_out.reshape(groups, exp_dev, slots_per, layer_width)
    cotangent_arrived = lax.all_to_all(cot_out, "expert", split_axis=0, concat_axis=0, tiled=True)
    back_proj = jnp.einsum(
        "pzot,zat->pzoa", cotangent_arrived, down_adapter_output, preferred_element_type=jnp.float32
    ).astype(jnp.bfloat16)
    partial_a = jnp.einsum("secr,secf->erf", back_proj, cached, preferred_element_type=jnp.float32)
    partial_b = jnp.einsum(
        "secr,secd->erd", projected_hidden, cotangent_arrived, preferred_element_type=jnp.float32
    )
    total_a, total_b = lax.psum((partial_a, partial_b), "dp")
    position_dp = lax.axis_index("dp")
    share_a = hidden_width // shards
    share_b = layer_width // shards
    grad_a = lax.dynamic_slice_in_dim(total_a, position_dp * share_a, share_a, 2)
    grad_b = lax.dynamic_slice_in_dim(total_b, position_dp * share_b, share_b, 2)
    return (grad_a, grad_b)


def solution(mesh):
    placed = (
        P(("dom", "dp"), None, "expert", None, None),
        P(("dom", "dp", "expert"), None),
        P(("dom", "dp", "expert"), None),
        P("expert", None, "dp"),
        P(("dom", "expert"), None, "dp"),
        P("expert", None, None),
        P(("dom", "expert"), None, None),
    )
    return jax.shard_map(
        on_device,
        mesh=mesh,
        in_specs=placed,
        out_specs=(P(("dom", "expert"), None, "dp"), P(("dom", "expert"), None, "dp")),
        check_vma=False,
    )
```

profile of v0, /device:TPU:0, one launch (start us, length us, event | category | flops | bytes accessed | tf_op | source)
XLA Modules:
  0.0 557.5 jit_solution(9738480308191688542)
XLA Ops:
  7.2 1.1 pad_maximum_fusion
  8.3 7.8 %all_gather.3 = bf16[2,64,1280]{2,1,0:T(8,128)(2,1)S(1)} all-gather(bf16[2,64,640]{2,1,0:T(8,128)(2,1)S(1)} %pad_maximum_fusion), channel_id=1, replica_groups=mesh['dom'=2,'dp'=2,'expert'=8] {'dp'}, dimensions={2}, use_global_device_ids=true | all-gather | bytes 491520 | tf_op jit(solution)/shard_map/all_gather | solution.py:24
  16.1 1.4 fusion.17
  17.5 3.5 convert_bitcast_fusion
  21.0 7.3 %copy.52 = bf16[8,2,66,3584]{3,1,2,0:T(2,128)(2,1)} copy(bf16[8,2,66,3584]{3,2,0,1:T(8,128)(2,1)S(1)} %convert_bitcast_fusion) | data formatting | bytes 15138816 | tf_op jit(solution)/shard_map/convert_element_type | solution.py:32
  28.3 5.3 all-to-all-start
  33.6 0.1 copy.43
  33.7 0.1 eq.29
  33.9 0.1 copy.42
  34.0 0.1 mul.49
  34.1 0.1 copy.47
  34.3 4.5 reduce-window.6
  38.9 0.1 copy.45
  39.4 4.3 scatter_custom_fusion.1
  43.7 0.1 broadcast_in_dim.37
  43.8 4.3 scatter_custom_fusion
  48.3 0.1 copy.50
  48.5 151.5 %all-to-all-done = bf16[8,2,66,3584]{3,1,2,0:T(2,128)(2,1)} async-done(((bf16[8,2,66,3584]{3,1,2,0:T(2,128)(2,1)}), bf16[8,2,66,3584]{3,1,2,0:T(2,128)(2,1)}, u32[]{:S(2)}, u32[]{:S(2)}) %all-to-all-start) | async-done | bytes 7569440 | tf_op jit(solution)/shard_map/all_to_all | solution.py:33
  200.0 7.9 %copy.53 = bf16[8,2,66,3584]{3,2,1,0:T(8,128)(2,1)} copy(bf16[8,2,66,3584]{3,1,2,0:T(2,128)(2,1)} %all-to-all-done) | data formatting | bytes 15138816 | tf_op jit(solution)/shard_map/all_to_all | solution.py:33
  207.8 7.5 %reshape.91 = bf16[1056,3584]{1,0:T(8,128)(2,1)} reshape(bf16[8,2,66,3584]{3,2,1,0:T(8,128)(2,1)} %copy.53) | data formatting | bytes 15138816 | tf_op jit(solution)/shard_map/reshape | solution.py:40
  215.3 17.9 %gather_fusion = bf16[1024,3584]{1,0:T(8,128)(2,1)} fusion(bf16[1056,3584]{1,0:T(8,128)(2,1)} %reshape.91, s32[1024]{0:T(1024)S(1)} %broadcast_clamp_fusion), kind=kCustom, calls=%fused_computation | custom fusion | bytes 14684160 | tf_op jit(solution)/shard_map/jit(_take)/gather | solution.py:41
  233.2 13.2 %multiply_reduce_fusion = f32[128,3584]{1,0:T(8,128)} fusion(bf16[1024,3584]{1,0:T(8,128)(2,1)} %gather_fusion, f32[128,8]{1,0:T(8,128)S(1)} %copy.47, pred[128,8]{1,0:T(8,128)(4,1)S(1)} %copy.50), kind=kLoop, calls=%fused_computation.5 | loop fusion | flops 14221312 | bytes 9180160 | tf_op jit(solution)/shard_map/reduce_sum | solution.py:42
  246.5 17.3 %gather_fusion.1 = f32[1056,3584]{1,0:T(8,128)} fusion(f32[128,3584]{1,0:T(8,128)} %multiply_reduce_fusion, s32[2048]{0:T(1024)S(1)} %pad_clamp_fusion), kind=kCustom, calls=%fused_computation.1 | custom fusion | bytes 30281856 | tf_op jit(solution)/shard_map/jit(_take)/gather | solution.py:47
  263.8 11.1 %gather.15 = f32[8,2,66,3584]{3,2,1,0:T(8,128)} reshape(f32[1056,3584]{1,0:T(8,128)} %gather_fusion.1) | data formatting | bytes 30277632 | tf_op jit(solution)/shard_map/jit(_take)/gather | solution.py:47
  274.9 7.3 %multiply_convert_fusion = bf16[8,2,66,3584]{3,2,1,0:T(8,128)(2,1)S(1)} fusion(f32[8,2,66,3584]{3,2,1,0:T(8,128)} %gather.15, f32[8,2,66]{2,1,0:T(2,128)S(1)} %mul.51, pred[8,2,66]{2,1,0:T(4,128)(4,1)S(1)} %broadcast_in_dim.37), kind=kLoop, calls=%fused_computation.4 | loop fusion | flops 11354112 | bytes 22713504 | tf_op jit(solution)/shard_map/convert_element_type | solution.py:47
  282.1 37.6 %copy.54 = bf16[8,2,66,3584]{3,1,2,0:T(2,128)(2,1)S(1)} copy(bf16[8,2,66,3584]{3,2,1,0:T(8,128)(2,1)S(1)} %multiply_convert_fusion) | data formatting | bytes 15138816 | tf_op jit(solution)/shard_map/convert_element_type | solution.py:47
  319.7 170.1 %all_to_all.10 = bf16[8,2,66,3584]{3,1,2,0:T(2,128)(2,1)} all-to-all(bf16[8,2,66,3584]{3,1,2,0:T(2,128)(2,1)S(1)} %copy.54), channel_id=1, replica_groups=mesh['dom'=2,'dp'=2,'expert'=8] {'expert'}, dimensions={0} | all-to-all | bytes 15138816 | tf_op jit(solution)/shard_map/all_to_all | solution.py:51
  489.8 8.1 %fusion.11 = f32[2,32,1280]{2,1,0:T(8,128)} fusion(bf16[8,2,66,1280]{3,1,2,0:T(2,128)(2,1)S(1)} %bitcast.59, bf16[8,2,66,3584]{3,1,2,0:T(2,128)(2,1)} %all_to_all.10, bf16[2,32,3584]{2,1,0:T(8,128)(2,1)S(1)} %copy-done.1), kind=kOutput, calls=%fused_computation.17 | convolution fusion | flops 328762368 | bytes 11059200 | tf_op jit(solution)/shard_map/secr,secf->erf/dot_general | solution.py:55
  497.9 6.0 %fusion.4 = f32[2,32,3584]{2,1,0:T(8,128)} fusion(bf16[8,2,66,3584]{3,1,2,0:T(2,128)(2,1)} %all_to_all.10, bf16[8,2,66,64]{2,3,0,1:T(8,128)(2,1)S(1)} %fusion.17), kind=kOutput, calls=%fused_computation.12 | convolution fusion | flops 242221056 | bytes 8617984 | tf_op jit(solution)/shard_map/secr,secd->erd/dot_general | solution.py:56
  503.9 43.3 %all-reduce.3.cloned.1.call-done = (f32[2,32,1280]{2,1,0:T(8,128)}, f32[2,32,3584]{2,1,0:T(8,128)}) async-done(((f32[2,32,1280]{2,1,0:T(8,128)}, f32[2,32,3584]{2,1,0:T(8,128)}), (f32[2,32,1280]{2,1,0:T(8,128)}, f32[2,32,3584]{2,1,0:T(8,128)})) %all-reduce.3.cloned.1.call-update) | async-done | bytes 1245200 | tf_op jit(solution)/shard_map/psum | solution.py:59
  547.2 1.6 constant_dynamic-slice_fusion
  548.8 1.8 constant_dynamic-slice_fusion.1
  (30 shorter events, 0.8 us)
Async XLA Ops:
  7.2 8.9 %copy-start = (bf16[1,8,2,66,1280]{4,2,3,1,0:T(2,128)(2,1)S(1)}, bf16[1,8,2,66,1280]{4,2,3,1,0:T(2,128)(2,1)}, u32[]{:S(2)}) copy-start(bf16[1,8,2,66,1280]{4,2,3,1,0:T(2,128)(2,1)} %param.7) | copy-start | bytes 8110084
  28.3 5.3 copy-start.2
  28.3 5.8 %copy-start.3 = (f32[128,8]{0,1:T(8,128)S(1)}, f32[128,8]{0,1:T(8,128)}, u32[]{:S(2)}) copy-start(f32[128,8]{0,1:T(8,128)} %param.9) | copy-start | bytes 12292
  28.3 171.7 %all-to-all-start = ((bf16[8,2,66,3584]{3,1,2,0:T(2,128)(2,1)}), bf16[8,2,66,3584]{3,1,2,0:T(2,128)(2,1)}, u32[]{:S(2)}, u32[]{:S(2)}) async-start(bf16[8,2,66,3584]{3,1,2,0:T(2,128)(2,1)} %copy.52), calls=%async_computation | async-start | bytes 15138816 | tf_op jit(solution)/shard_map/all_to_all | solution.py:33
  33.5 513.7 %all-reduce.3.cloned.1.call-start = ((), (), s32[]{:S(2)}) async-start(), calls=%async_computation.2 | async-start | bytes 2490368 | tf_op jit(solution)/shard_map/psum | solution.py:59
  319.7 170.1 %copy-start.1 = (bf16[2,32,3584]{2,1,0:T(8,128)(2,1)S(1)}, bf16[2,32,3584]{2,1,0:T(8,128)(2,1)}, u32[]{:S(2)}) copy-start(bf16[2,32,3584]{2,1,0:T(8,128)(2,1)} %param.12) | copy-start | bytes 1376260
Sparse Core Ops, SparseCore 0:
  504.0 43.1 all-reduce.2
where the time goes:
time: 558 us; the launch traced here: 557 us
  waiting for transfers between devices  195 us (35%)
  blocking collectives  178 us (32%)
  local copies, waits for them, and re-layouts  120 us (22%)
  other arithmetic  26.3 us (5%)
  matrix products  19 us (3%)
  between operations  14.2 us (3%)
    all_to_all x1, blocking collectives, on_device(): lax.all_to_all(cot_out, 'expert', split_axis=0, concat_axis=0, tiled=True)  170 us
    all_to_all x1, waiting for transfers between devices, on_device(): lax.all_to_all(tangent_row_block, 'expert', split_axis=0, concat_axis=0,...  151 us
    psum x1, waiting for transfers between devices, on_device(): total_a, total_b = lax.psum((partial_a, partial_b), 'dp')  43.3 us
    convert_element_type x1, local copies, waits for them, and re-layouts, on_device(): (slot_gate[:, None] * jnp.take(output_tangent, slot_token, axis=0)).astyp...  37.6 us
    gather x2, local copies, waits for them, and re-layouts, on_device(): jnp.take(output_tangent, slot_token, axis=0)  28.4 us
    gather x1, local copies, waits for them, and re-layouts, on_device(): jnp.take(returned_flat, positions, axis=0)  17.9 us
    reduce_sum x1, other arithmetic, on_device(): jnp.sum(gates[:, :, None] * picked.astype(jnp.float32), axis=1)  13.2 us
  transfers between devices with their start and end apart: 2, of which 2 were waited for; matrix products, arithmetic and copies ran while one was open for 3% of the time, Pallas kernels for 0%

commit v1 on v0

v1 whole, which is shorter than its diff:
```python
import jax
import jax.numpy as jnp
from jax import lax
from jax.sharding import PartitionSpec as P

F32 = jnp.float32
BF16 = jnp.bfloat16


def split_two(x):
    high = x.astype(BF16)
    low = (x - high.astype(F32)).astype(BF16)
    return high, low


def routing_tables(expert_choice_index, gates, experts):
    labels = jnp.arange(experts, dtype=jnp.int32)
    matches = expert_choice_index[:, :, None] == labels[None, None, :]
    weight = jnp.sum(jnp.where(matches, gates[:, :, None], 0.0), axis=1)
    chosen = jnp.any(matches, axis=1)
    tokens = expert_choice_index.shape[0]
    earlier = jnp.tril(jnp.ones((tokens, tokens), BF16), -1)
    before = jnp.dot(earlier, chosen.astype(BF16), preferred_element_type=F32)
    position = jnp.where(chosen, before, -1.0)
    return position, weight


def on_device(
    hidden,
    expert_choice_index,
    gates,
    down_adapter_hidden,
    hidden_tangent,
    down_adapter_output,
    output_tangent_factor,
):
    cached = hidden[0]
    groups, exp_dev, slots_per, hidden_width = cached.shape
    rank = down_adapter_output.shape[1]
    layer_width = down_adapter_output.shape[2]
    shards = lax.axis_size("dp")
    experts = groups * exp_dev
    share_a = hidden_width // shards
    share_b = layer_width // shards
    me = lax.axis_index("expert")
    dp = lax.axis_index("dp")

    adapter_pieces = jnp.concatenate([down_adapter_hidden, hidden_tangent], axis=1)
    adapter_set = lax.all_gather(adapter_pieces, "dp", axis=2, tiled=True)
    stacked = jnp.concatenate([output_tangent_factor, down_adapter_output], axis=1)
    stacked_share = lax.dynamic_slice_in_dim(stacked, dp * share_b, share_b, 2)
    factors = lax.all_gather(stacked_share, "expert", axis=0, tiled=True)
    factors = factors.reshape(experts * 2 * rank, share_b)

    position, weight = routing_tables(expert_choice_index, gates, experts)
    tables = lax.all_gather(jnp.concatenate([position, weight], axis=1), "expert", axis=0)
    position, weight = tables[:, :, :experts], tables[:, :, experts:]

    projected = jnp.einsum("secf,erf->secr", cached, adapter_set, preferred_element_type=F32)
    projected = lax.all_gather(projected.astype(BF16), "expert", axis=1, tiled=True)
    places = jnp.arange(slots_per, dtype=jnp.int32).astype(F32)
    onehot = (position[:, :, :, None] == places).astype(BF16)
    rows = jnp.einsum("stxc,sxcr->stxr", onehot, projected, preferred_element_type=F32)
    rows = weight[:, :, :, None] * rows
    tokens = rows.shape[0] * rows.shape[1]
    mine = lax.dynamic_slice_in_dim(rows, me * exp_dev, exp_dev, 2)[..., :rank]
    mine = mine.reshape(tokens, exp_dev * rank)
    rows = rows.reshape(tokens, experts * 2 * rank)
    rows_b = rows.astype(BF16)

    mixing = jnp.einsum("na,nb->ab", mine.astype(BF16), rows_b, preferred_element_type=F32)
    own_output = lax.dynamic_slice_in_dim(down_adapter_output, dp * share_b, share_b, 2)
    gram = jnp.einsum(
        "rm,eam->rea", factors, own_output, preferred_element_type=F32
    ).reshape(experts * 2 * rank, exp_dev * rank)
    gram, mixing = lax.psum((gram, mixing), "dp")

    high, low = split_two(mixing)
    grad_b = jnp.dot(high, factors, preferred_element_type=F32)
    grad_b = grad_b + jnp.dot(low, factors, preferred_element_type=F32)
    grad_b = grad_b.reshape(exp_dev, rank, share_b)

    back = jnp.dot(rows_b, gram.astype(BF16), preferred_element_type=F32)
    back = back.reshape(groups, -1, exp_dev, rank)
    own_weight = lax.dynamic_slice_in_dim(weight, me * exp_dev, exp_dev, 2)
    back = (back * own_weight[..., None]).astype(BF16)
    own_onehot = lax.dynamic_slice_in_dim(onehot, me * exp_dev, exp_dev, 2)
    back_slots = jnp.einsum(
        "stec,ster->secr", own_onehot, back, preferred_element_type=F32
    ).astype(BF16)
    part_a = jnp.einsum("secr,secf->erf", back_slots, cached, preferred_element_type=F32)
    grad_a = lax.psum_scatter(part_a, "dp", scatter_dimension=2, tiled=True)
    return (grad_a, grad_b)


def solution(mesh):
    placed = (
        P(("dom", "dp"), None, "expert", None, None),
        P(("dom", "dp", "expert"), None),
        P(("dom", "dp", "expert"), None),
        P("expert", None, "dp"),
        P(("dom", "expert"), None, "dp"),
        P("expert", None, None),
        P(("dom", "expert"), None, None),
    )
    return jax.shard_map(
        on_device,
        mesh=mesh,
        in_specs=placed,
        out_specs=(P(("dom", "expert"), None, "dp"), P(("dom", "expert"), None, "dp")),
        check_vma=False,
    )
```

time: 558 us -> 142 us (0.25)
  blocking collectives: 178 us -> 37.8 us
  waiting for transfers between devices: 195 us -> 64.5 us
  local copies, waits for them, and re-layouts: 120 us -> 2.23 us
  other arithmetic: 26.3 us -> 4.65 us
    all_to_all x1 -> x0, blocking collectives: 170 us -> none  [on_device(): lax.all_to_all(cot_out, 'expert', split_axis=0, concat_axis=0, tiled=True)]
    all_to_all x1 -> x0, waiting for transfers between devices: 151 us -> none  [on_device(): lax.all_to_all(tangent_row_block, 'expert', split_axis=0, concat_axis=0,...]
    all_gather x0 -> x2, waiting for transfers between devices: none -> 50.6 us  [the longest x1 38.5 us: on_device(): factors = lax.all_gather(stacked_share, 'expert', axis=0, tiled=True)]
    gather x3 -> x0, local copies, waits for them, and re-layouts: 46.3 us -> none  [the longest x2 28.4 us: on_device(): jnp.take(output_tangent, slot_token, axis=0)]
    convert_element_type x2 -> x1, local copies, waits for them, and re-layouts: 44.8 us -> 1.79 us  [on_device(): rows_b = rows.astype(BF16)]
    psum x1, waiting for transfers between devices: 43.3 us -> 3.33 us  [on_device(): gram, mixing = lax.psum((gram, mixing), 'dp')]
    psum x0 -> x1, blocking collectives: none -> 15.2 us  [on_device(): gram, mixing = lax.psum((gram, mixing), 'dp')]
    all_gather x0 -> x1, blocking collectives: none -> 14.7 us  [on_device(): lax.all_gather(jnp.concatenate([position, weight], axis=1), 'expert', axi...]
  transfers between devices with their start and end apart: 2 -> 4, of which waited for: 2 -> 4; matrix products, arithmetic and copies ran while one was open for 3% -> 16% of each run, Pallas kernels for 0% -> 0%
where the time goes in v1:
time: 142 us
  waiting for transfers between devices  64.5 us (45%)
  blocking collectives  37.8 us (27%)
  matrix products  18.9 us (13%)
  between operations  14 us (10%)
  other arithmetic  4.65 us (3%)
  local copies, waits for them, and re-layouts  2.23 us (2%)
    all_gather x1, waiting for transfers between devices, on_device(): factors = lax.all_gather(stacked_share, 'expert', axis=0, tiled=True)  38.5 us
    psum x1, blocking collectives, on_device(): gram, mixing = lax.psum((gram, mixing), 'dp')  15.2 us
    all_gather x1, blocking collectives, on_device(): lax.all_gather(jnp.concatenate([position, weight], axis=1), 'expert', axi...  14.7 us
    all_gather x1, waiting for transfers between devices, on_device(): lax.all_gather(projected.astype(BF16), 'expert', axis=1, tiled=True)  12.2 us
    reduce_scatter x1, waiting for transfers between devices, on_device(): grad_a = lax.psum_scatter(part_a, 'dp', scatter_dimension=2, tiled=True)  10.4 us
    all_gather x1, blocking collectives, on_device(): adapter_set = lax.all_gather(adapter_pieces, 'dp', axis=2, tiled=True)  7.8 us
    psum x1, waiting for transfers between devices, on_device(): gram, mixing = lax.psum((gram, mixing), 'dp')  3.33 us
    dot_general x1, matrix products, on_device(): jnp.einsum('rm,eam->rea', factors, own_output, preferred_element_type=F32)  3.25 us
  transfers between devices with their start and end apart: 4, of which 4 were waited for; matrix products, arithmetic and copies ran while one was open for 16% of the time, Pallas kernels for 0%

profile of v1, /device:TPU:0, one launch (start us, length us, event | category | flops | bytes accessed | tf_op | source)
XLA Modules:
  0.0 142.1 jit_solution(1012361650842202445)
XLA Ops:
  7.2 0.0 copy-start
  7.2 0.0 all-gather.4.cloned.1.call-start
  7.2 1.1 pad_maximum_fusion
  8.3 7.8 %all_gather.17 = bf16[2,64,1280]{2,1,0:T(8,128)(2,1)S(1)} all-gather(bf16[2,64,640]{2,1,0:T(8,128)(2,1)S(1)} %pad_maximum_fusion), channel_id=1, replica_groups=mesh['dom'=2,'dp'=2,'expert'=8] {'dp'}, dimensions={2}, use_global_device_ids=true | all-gather | bytes 491520 | tf_op jit(solution)/shard_map/all_gather | solution.py:49
  16.1 2.1 %fusion.17 = bf16[8,2,66,64]{2,3,1,0:T(8,128)(2,1)} fusion(bf16[8,2,66,1280]{3,1,2,0:T(2,128)(2,1)S(1)} %bitcast.50, bf16[2,64,1280]{2,1,0:T(8,128)(2,1)S(1)} %all_gather.17), kind=kOutput, calls=%fused_computation.15 | convolution fusion | flops 173082624 | bytes 3166208 | tf_op jit(solution)/shard_map/secf,erf->secr/dot_general | solution.py:59
  18.3 0.0 all-gather.4.cloned.1.call-update
  18.3 0.0 all-gather.6.cloned.1.call-start
  18.4 1.7 %fusion.23 = bf16[2,64,1792]{2,1,0:T(8,128)(2,1)} fusion(s32[]{:T(128)S(6)} %select_n.25, bf16[2,32,3584]{2,1,0:T(8,128)(2,1)} %param.13, bf16[2,32,3584]{2,1,0:T(8,128)(2,1)S(1)} %copy-done.4), kind=kLoop, calls=%fused_computation.22 | loop fusion | flops 917504 | bytes 1376260 | tf_op jit(solution)/shard_map/concatenate | solution.py:50
  20.1 0.0 all-gather.6.cloned.1.call-update
  20.1 0.0 all-reduce.3.cloned.1.call-start
  20.3 0.2 convolution_select_fusion
  20.5 14.7 %all-gather = f32[1024,32]{0,1:T(8,128)S(1)} all-gather(f32[128,32]{0,1:T(8,128)S(1)} %pad_maximum_fusion.1), channel_id=2, replica_groups=mesh['dom'=2,'dp'=2,'expert'=8] {'expert'}, dimensions={0}, use_global_device_ids=true | all-gather | bytes 147456 | tf_op jit(solution)/shard_map/all_gather | solution.py:56
  35.3 1.8 %broadcast_compare_fusion = pred[8,128,16,66]{1,3,0,2:T(8,128)(4,1)} fusion(f32[8,128,16]{1,0,2:T(8,128)S(1)} %get-tuple-element.3, f32[66]{0:T(128)S(1)} %iota_convert_fusion), kind=kLoop, calls=%fused_computation.7 | loop fusion | flops 1081344 | bytes 1147144 | tf_op jit(solution)/shard_map/eq | solution.py:62
  37.1 12.2 %all-gather.4.cloned.1.call-done = bf16[8,16,66,64]{2,3,1,0:T(8,128)(2,1)} async-done(((bf16[8,2,66,64]{2,3,1,0:T(8,128)(2,1)}), bf16[8,16,66,64]{2,3,1,0:T(8,128)(2,1)}) %all-gather.4.cloned.1.call-update) | async-done | bytes 1081360 | tf_op jit(solution)/shard_map/all_gather | solution.py:60
  49.3 2.7 %bitcast_multiply_fusion = bf16[8,128,16,64]{1,3,2,0:T(8,128)(2,1)S(1)} fusion(bf16[8,16,66,64]{2,3,1,0:T(8,128)(2,1)} %all-gather.4.cloned.1.call-done, f32[8,128,16]{1,2,0:T(8,128)S(1)} %copy.34, f32[8,128,16]{1,0,2:T(8,128)S(1)} %get-tuple-element.3, f32[66]{0:T(128)S(1)} %iota_convert_fusion), kind=kOutput, calls=%fused_computation.2 | convolution fusion | flops 141590528 | bytes 3309832 | tf_op jit(solution)/shard_map/stxc,sxcr->stxr/dot_general | solution.py:63
  52.0 1.8 %copy.42 = bf16[8,128,16,64]{1,0,3,2:T(8,128)(2,1)S(1)} copy(bf16[8,128,16,64]{1,3,2,0:T(8,128)(2,1)S(1)} %bitcast_multiply_fusion) | data formatting | bytes 4194304 | tf_op jit(solution)/shard_map/convert_element_type | solution.py:69
  53.8 0.1 copy.41
  53.9 1.5 %fusion.11 = f32[64,1024]{1,0:T(8,128)} fusion(bf16[128,8,8,128]{3,2,1,0:T(8,128)(2,1)S(1)} %bitcast.56, bf16[8,8,8,128]{3,2,1,0:T(8,128)(2,1)S(1)} %bitcast.62), kind=kOutput, calls=%fused_computation.10 | convolution fusion | flops 134217728 | bytes 2490368 | tf_op jit(solution)/shard_map/na,nb->ab/dot_general | solution.py:71
  55.4 0.0 all-reduce.3.cloned.1.call-update
  55.4 0.0 reduce-scatter.2.cloned.1.call-start
  55.4 38.5 %all-gather.6.cloned.1.call-done = bf16[16,64,1792]{2,1,0:T(8,128)(2,1)} async-done(((bf16[2,64,1792]{2,1,0:T(8,128)(2,1)}), bf16[16,64,1792]{2,1,0:T(8,128)(2,1)}) %all-gather.6.cloned.1.call-update) | async-done | bytes 3670032 | tf_op jit(solution)/shard_map/all_gather | solution.py:52
  93.9 3.2 %fusion.43 = f32[1024,64]{0,1:T(8,128)S(1)} fusion(bf16[1024,1792]{1,0:T(8,128)(2,1)} %bitcast.52, bf16[64,1792]{1,0:T(8,128)(2,1)S(1)} %bitcast.57), kind=kOutput, calls=%fused_computation.50 | convolution fusion | flops 234881024 | bytes 4161536 | tf_op jit(solution)/shard_map/rm,eam->rea/dot_general | solution.py:73
  97.2 15.2 %all-reduce.4 = bf16[1024,64]{0,1:T(8,128)(2,1)S(1)} all-reduce(f32[1024,64]{0,1:T(8,128)S(1)} %fusion.43), channel_id=1, replica_groups=mesh['dom'=2,'dp'=2,'expert'=8] {'dp'}, use_global_device_ids=true, to_apply=%region_2.3 | all-reduce | flops 65536 | bytes 393216 | tf_op jit(solution)/shard_map/psum | solution.py:76
  112.4 2.1 %fusion.20 = bf16[8,128,2,32]{1,3,2,0:T(8,128)(2,1)S(1)} fusion(bf16[8,128,1024,1]{1,2,3,0:T(8,128)(2,1)} %bitcast.55, bf16[2,32,1024,1]{2,1,0,3:T(8,128)(2,1)S(1)} %bitcast.58, f32[8,128,2]{1,2,0:T(2,128)S(1)} %copy.38), kind=kOutput, calls=%fused_computation.16 | convolution fusion | flops 134348800 | bytes 2367488 | tf_op jit(solution)/shard_map/dot_general | solution.py:83
  114.5 2.5 %fusion.6 = f32[2,32,1280]{2,1,0:T(8,128)} fusion(bf16[8,2,66,1280]{3,1,2,0:T(2,128)(2,1)S(1)} %bitcast.51, pred[8,128,16,66]{1,3,0,2:T(8,128)(4,1)} %broadcast_compare_fusion, s32[]{:T(128)S(6)} %select_n.24, bf16[8,128,2,32]{1,3,2,0:T(8,128)(2,1)S(1)} %fusion.20), kind=kOutput, calls=%fused_computation.9 | convolution fusion | flops 95192064 | bytes 3309572 | tf_op jit(solution)/shard_map/secr,secf->erf/dot_general | solution.py:91
  117.0 0.0 reduce-scatter.2.cloned.1.call-update
  117.0 3.3 %all-reduce.3.cloned.1.call-done = f32[64,1024]{1,0:T(8,128)} async-done(((f32[64,1024]{1,0:T(8,128)}), f32[64,1024]{1,0:T(8,128)}) %all-reduce.3.cloned.1.call-update) | async-done | bytes 262160 | tf_op jit(solution)/shard_map/psum | solution.py:76
  120.4 3.0 %fusion.30 = f32[64,1792]{1,0:T(8,128)S(1)} fusion(bf16[1024,1792]{1,0:T(8,128)(2,1)} %bitcast.53, f32[64,1024]{1,0:T(8,128)} %all-reduce.3.cloned.1.call-done), kind=kOutput, calls=%fused_computation.31 | convolution fusion | flops 234946560 | bytes 4390912 | tf_op jit(solution)/shard_map/dot_general | solution.py:79
  123.4 0.2 copy-done.1
  123.6 0.0 copy-done.3
  123.6 1.5 %convolution_add_fusion = f32[64,1792]{1,0:T(8,128)} fusion(f32[64,1792]{1,0:T(8,128)S(1)} %fusion.30, bf16[1024,1792]{1,0:T(8,128)(2,1)S(1)} %bitcast.54, f32[64,1024]{1,0:T(8,128)S(1)} %copy-done.3), kind=kOutput, calls=%fused_computation.8 | convolution fusion | flops 235257856 | bytes 4849664 | tf_op jit(solution)/shard_map/dot_general | solution.py:80
  125.1 10.4 %reduce-scatter.2.cloned.1.call-done = f32[2,32,640]{2,1,0:T(8,128)} async-done(((f32[2,32,1280]{2,1,0:T(8,128)}), f32[2,32,640]{2,1,0:T(8,128)}) %reduce-scatter.2.cloned.1.call-update) | async-done | bytes 163856 | tf_op jit(solution)/shard_map/reduce_scatter | solution.py:92
  (23 shorter events, 0.2 us)
Async XLA Ops:
  7.2 9.0 %copy-start = (bf16[1,8,2,66,1280]{4,2,3,1,0:T(2,128)(2,1)S(1)}, bf16[1,8,2,66,1280]{4,2,3,1,0:T(2,128)(2,1)}, u32[]{:S(2)}) copy-start(bf16[1,8,2,66,1280]{4,2,3,1,0:T(2,128)(2,1)} %param.7) | copy-start | bytes 8110084
  7.2 11.2 %copy-start.4 = (bf16[2,32,3584]{2,1,0:T(8,128)(2,1)S(1)}, bf16[2,32,3584]{2,1,0:T(8,128)(2,1)}, u32[]{:S(2)}) copy-start(bf16[2,32,3584]{2,1,0:T(8,128)(2,1)} %param.12) | copy-start | bytes 1376260
  7.2 42.1 %all-gather.4.cloned.1.call-start = ((), (), s32[]{:S(2)}) async-start(), calls=%async_computation.1 | async-start | bytes 2359296 | tf_op jit(solution)/shard_map/all_gather | solution.py:60
  16.1 4.1 %copy-start.5 = (s32[128,8]{0,1:T(8,128)S(1)}, s32[128,8]{0,1:T(8,128)}, u32[]{:S(2)}) copy-start(s32[128,8]{0,1:T(8,128)} %param.8) | copy-start | bytes 12292
  16.1 4.1 %copy-start.6 = (f32[128,8]{0,1:T(8,128)S(1)}, f32[128,8]{0,1:T(8,128)}, u32[]{:S(2)}) copy-start(f32[128,8]{0,1:T(8,128)} %param.9) | copy-start | bytes 12292
  18.3 75.6 %all-gather.6.cloned.1.call-start = ((), (), s32[]{:S(2)}) async-start(), calls=%async_computation.2 | async-start | bytes 4128768 | tf_op jit(solution)/shard_map/all_gather | solution.py:52
  20.1 100.2 %all-reduce.3.cloned.1.call-start = ((), (), s32[]{:S(2)}) async-start(), calls=%async_computation.4 | async-start | bytes 524288 | tf_op jit(solution)/shard_map/psum | solution.py:76
  52.0 1.8 %copy-start.2 = (bf16[8,128,16,64]{1,3,2,0:T(8,128)(2,1)}, bf16[8,128,16,64]{1,3,2,0:T(8,128)(2,1)S(1)}, u32[]{:S(2)}) copy-start(bf16[8,128,16,64]{1,3,2,0:T(8,128)(2,1)S(1)} %bitcast_multiply_fusion) | copy-start | bytes 6291460
  55.4 80.2 %reduce-scatter.2.cloned.1.call-start = ((), (), s32[]{:S(2)}) async-start(), calls=%async_computation.3 | async-start | bytes 491520 | tf_op jit(solution)/shard_map/reduce_scatter | solution.py:92
  120.4 3.2 %copy-start.1 = (bf16[16,64,1792]{2,1,0:T(8,128)(2,1)S(1)}, bf16[16,64,1792]{2,1,0:T(8,128)(2,1)}, u32[]{:S(2)}) copy-start(bf16[16,64,1792]{2,1,0:T(8,128)(2,1)} %all-gather.6.cloned.1.call-done) | copy-start | bytes 11010052
  120.4 3.2 %copy-start.3 = (f32[64,1024]{1,0:T(8,128)S(1)}, f32[64,1024]{1,0:T(8,128)}, u32[]{:S(2)}) copy-start(f32[64,1024]{1,0:T(8,128)} %all-reduce.3.cloned.1.call-done) | copy-start | bytes 786436
Sparse Core Ops, SparseCore 0:
  18.4 30.8 all-gather.3
  51.5 42.3 all-gather.5
  96.2 24.1 all-reduce.2
  123.1 12.3 reduce-scatter.1

commit v2 on v1

--- a/solution.py
+++ b/solution.py
@@ -1,10 +1,15 @@
+import functools
+
 import jax
 import jax.numpy as jnp
 from jax import lax
+from jax.experimental import pallas as pl
+from jax.experimental.pallas import tpu as pltpu
 from jax.sharding import PartitionSpec as P
 
 F32 = jnp.float32
 BF16 = jnp.bfloat16
+MESH = pl.DeviceIdType.MESH
 
 
 def split_two(x):
@@ -25,7 +30,7 @@
     return position, weight
 
 
-def on_device(
+def on_device_collectives(
     hidden,
     expert_choice_index,
     gates,
@@ -93,6 +98,324 @@
     return (grad_a, grad_b)
 
 
+NT = (((1,), (1,)), ((), ()))
+TN = (((0,), (0,)), ((), ()))
+
+
+def dot(a, b, dims=(((1,), (0,)), ((), ()))):
+    return lax.dot_general(a, b, dims, preferred_element_type=F32)
+
+
+def fused_kernel(
+    n, rank, slots,
+    hidden, own_factors, own_adapters, own_table,
+    grad_a, grad_b,
+    factors, adapters, tables, proj_wide, proj, rows_of,
+    g_high, g_low, mix, mix_core, mix_sum, mix_dp, gram, gram_core, gram_sum, gram_dp,
+    back, pa, pa_in, gb, gb_in,
+    f_send, f_recv, p_send, p_recv, t_send, t_recv, m_send, m_recv, local,
+):
+    me = lax.axis_index("expert")
+    x = lax.axis_index("dp")
+    core = lax.rem(me, 2)
+    chip = me // 2
+    blocks = hidden.shape[0]
+    half = blocks // 2
+    padded = proj.shape[1]
+    experts = 2 * n
+    wide = factors.shape[2]
+    share = 2 * wide
+    depth = own_adapters.shape[1]
+    tokens = tables.shape[2]
+    two = 2 * rank
+    pair = 2 * two
+    quad = 4 * rank
+
+    barrier = pltpu.get_barrier_semaphore()
+    for d in range(1, n):
+        pl.semaphore_signal(
+            barrier, inc=1, device_id={"expert": lax.rem(me + d, n)}, device_id_type=MESH
+        )
+    pl.semaphore_signal(barrier, inc=1, device_id={"dp": 1 - x}, device_id_type=MESH)
+    pl.semaphore_wait(barrier, n)
+
+    def to_dp(k, src, dst):
+        return pltpu.make_async_remote_copy(
+            src_ref=src, dst_ref=dst, send_sem=m_send.at[k], recv_sem=m_recv.at[k],
+            device_id={"dp": 1 - x}, device_id_type=MESH,
+        )
+
+    def to_core(k, src, dst):
+        return pltpu.make_async_remote_copy(
+            src_ref=src, dst_ref=dst, send_sem=m_send.at[k], recv_sem=m_recv.at[k],
+            device_id={"expert": me + 1 - 2 * core}, device_id_type=MESH,
+        )
+
+    def to_peer(d, src, dst, send, recv):
+        return pltpu.make_async_remote_copy(
+            src_ref=src, dst_ref=dst, send_sem=send.at[d], recv_sem=recv.at[d],
+            device_id={"expert": lax.rem(me + d, n)}, device_id_type=MESH,
+        )
+
+    def columns_of(c):
+        return pl.ds(pl.multiple_of(x * share + c * wide, 128), wide)
+
+    adapter_copy = to_dp(0, own_adapters, adapters)
+    adapter_copy.start()
+    t_copies, f_copies, p_copies = {}, {}, {}
+    for d in range(1, n):
+        t_copies[d] = to_peer(d, own_table, tables.at[me], t_send, t_recv)
+        t_copies[d].start()
+        c_to = lax.rem(me + d, 2)
+        f_copies[d] = to_peer(d, own_factors.at[:, columns_of(c_to)], factors.at[me], f_send, f_recv)
+        p_copies[d] = to_peer(d, proj.at[pl.ds(half * c_to, half)], rows_of.at[me], p_send, p_recv)
+    order = [d for k in range(1, n // 2 + 1) for d in sorted({k, n - k})]
+    early = order[: max(1, n // 2 - 1)]
+    late = [d for d in order if d not in early]
+    for d in early:
+        f_copies[d].start()
+    f_local = pltpu.make_async_copy(own_factors.at[:, columns_of(core)], factors.at[me], local.at[0])
+    f_local.start()
+    t_local = pltpu.make_async_copy(own_table, tables.at[me], local.at[1])
+    t_local.start()
+
+    proj_wide[...] = jnp.zeros_like(proj_wide)
+    own_cols = pl.ds(pl.multiple_of(x * depth, 128), depth)
+    far_cols = pl.ds(pl.multiple_of((1 - x) * depth, 128), depth)
+    for s in range(blocks):
+        parts = [
+            dot(hidden[s, j, :, own_cols], own_adapters[j * two:(j + 1) * two, :], NT)
+            for j in range(2)
+        ]
+        proj_wide[s, 0:slots, :] = jnp.concatenate(parts, axis=1)
+    adapter_copy.wait_recv()
+    for s in range(blocks):
+        parts = [
+            dot(hidden[s, j, :, far_cols], adapters[j * two:(j + 1) * two, :], NT)
+            for j in range(2)
+        ]
+        proj_wide[s, 0:slots, :] = proj_wide[s, 0:slots, :] + jnp.concatenate(parts, axis=1)
+        proj[s] = proj_wide[s].astype(BF16)
+    for d in order:
+        p_copies[d].start()
+    for d in late:
+        f_copies[d].start()
+    p_local = pltpu.make_async_copy(proj.at[pl.ds(half * core, half)], rows_of.at[me], local.at[2])
+    p_local.start()
+
+    places = lax.broadcasted_iota(jnp.int32, (padded, tokens), 0).astype(F32)
+
+    def onehot(position):
+        return jnp.where(places == position, 1.0, 0.0).astype(BF16)
+
+    t_local.wait()
+    for d in range(1, n):
+        t_copies[d].wait_recv()
+    p_local.wait()
+    for d in range(0, n):
+        if d:
+            p_copies[d].wait_recv()
+        q = lax.rem(me + n - d, n)
+        for t in range(half):
+            block = half * core + t
+            marks = jnp.concatenate(
+                [onehot(tables[block, pl.ds(2 * q + j, 1), :]) for j in range(2)], axis=1
+            )
+            both = dot(rows_of[q, t], marks, TN)
+            for j in range(2):
+                weight = tables[block, pl.ds(experts + 2 * q + j, 1), :]
+                piece = both[j * two:(j + 1) * two, j * tokens:(j + 1) * tokens] * weight
+                high = piece.astype(BF16)
+                where = pl.ds(pl.multiple_of(q * pair + j * two, two), two)
+                g_high[where, t * tokens:(t + 1) * tokens] = high
+                g_low[where, t * tokens:(t + 1) * tokens] = (piece - high.astype(F32)).astype(BF16)
+
+    def chip_rows(ref, offset):
+        return jnp.concatenate(
+            [
+                ref[pl.ds(pl.multiple_of(chip * 4 * two + i * two + offset, rank), rank), :]
+                for i in range(4)
+            ],
+            axis=0,
+        )
+
+    a_high = chip_rows(g_high, 0)
+    a_low = chip_rows(g_low, 0)
+    a_both = jnp.concatenate([a_high, a_low], axis=0)
+    tile = 2 * pair
+    for r in range(0, experts * two, tile):
+        first = dot(a_both, g_high[r:r + tile, :], NT)
+        second = dot(a_high, g_low[r:r + tile, :], NT)
+        mix[:, r:r + tile] = first[:quad] + first[quad:] + second
+    mix_copy = to_core(1, mix, mix_core)
+    mix_copy.start()
+    mix_copy.wait_recv()
+    mix_sum[...] = mix[...] + mix_core[...]
+    mix_dp_copy = to_dp(2, mix_sum, mix_dp)
+    mix_dp_copy.start()
+
+    f_local.wait()
+    sibling = me + 1 - 2 * core
+    waited = set()
+    f_copies[1].wait_recv()
+    f_copies[n - 1].wait_recv()
+    waited = {0, 1, n - 1}
+    outs = jnp.concatenate(
+        [
+            factors[2 * chip + i, j * two + rank:(j + 1) * two, :]
+            for i in range(2)
+            for j in range(2)
+        ],
+        axis=0,
+    )
+    for d in [0] + order:
+        if d not in waited:
+            f_copies[d].wait_recv()
+        q = lax.rem(me + n - d, n)
+        gram[:, pl.ds(pl.multiple_of(q * pair, pair), pair)] = dot(outs, factors[q], NT)
+    gram_copy = to_core(3, gram, gram_core)
+    gram_copy.start()
+    gram_copy.wait_recv()
+    gram_sum[...] = gram[...] + gram_core[...]
+    gram_dp_copy = to_dp(4, gram_sum, gram_dp)
+    gram_dp_copy.start()
+
+    mix_dp_copy.wait_recv()
+    m_high, m_low = split_two(mix_sum[...] + mix_dp[...])
+    m_both = jnp.concatenate([m_high, m_low], axis=0)
+    total = None
+    for q in range(n):
+        term = dot(m_both[:, q * pair:(q + 1) * pair], factors[q])
+        total = term if total is None else total + term
+    gb[...] = total[:quad] + total[quad:]
+    gb_copy = to_core(5, gb.at[pl.ds(pl.multiple_of((1 - core) * two, two), two)], gb_in)
+    gb_copy.start()
+    mine = pl.ds(pl.multiple_of(core * wide, 128), wide)
+    other = pl.ds(pl.multiple_of((1 - core) * wide, 128), wide)
+    grad_b[:, mine] = gb[pl.ds(pl.multiple_of(core * two, two), two), :]
+
+    gram_dp_copy.wait_recv()
+    k_high, k_low = split_two(gram_sum[...] + gram_dp[...])
+    k_both = jnp.concatenate([k_high, k_low], axis=0)
+    for t in range(half):
+        cols = slice(t * tokens, (t + 1) * tokens)
+        first = dot(k_both, g_high[:, cols])
+        value = first[:quad] + first[quad:] + dot(k_high, g_low[:, cols])
+        block = half * core + t
+        for i in range(4):
+            weight = tables[block, pl.ds(experts + 4 * chip + i, 1), :]
+            piece = value[i * rank:(i + 1) * rank] * weight
+            back[core, i * rank:(i + 1) * rank, cols] = piece.astype(BF16)
+    back_copy = to_core(
+        6,
+        back.at[core, pl.ds(pl.multiple_of((1 - core) * two, two), two)],
+        back.at[core, pl.ds(pl.multiple_of((1 - core) * two, two), two)],
+    )
+    back_copy.start()
+    back_copy.wait_recv()
+    for j in range(2):
+        acc = None
+        for s in range(blocks):
+            t = s % half
+            rows = back[
+                s // half,
+                pl.ds(pl.multiple_of(core * two + j * rank, rank), rank),
+                t * tokens:(t + 1) * tokens,
+            ]
+            placed = dot(rows, onehot(tables[s, pl.ds(2 * me + j, 1), :]), NT).astype(BF16)
+            term = dot(placed[:, :slots], hidden[s, j])
+            acc = term if acc is None else acc + term
+        for h in range(2):
+            pa[h, j * rank:(j + 1) * rank, :] = acc[:, h * depth:(h + 1) * depth]
+    pa_copy = to_dp(7, pa.at[1 - x], pa_in)
+    pa_copy.start()
+    gb_copy.wait_recv()
+    grad_b[:, other] = gb_in[...]
+    pa_copy.wait_recv()
+    grad_a[...] = pa[x] + pa_in[...]
+
+    for d in range(1, n):
+        t_copies[d].wait_send()
+        f_copies[d].wait_send()
+        p_copies[d].wait_send()
+    for copy in (
+        adapter_copy, mix_copy, mix_dp_copy, gram_copy, gram_dp_copy, gb_copy, back_copy, pa_copy
+    ):
+        copy.wait_send()
+
+
+def on_device(
+    hidden,
+    expert_choice_index,
+    gates,
+    down_adapter_hidden,
+    hidden_tangent,
+    down_adapter_output,
+    output_tangent_factor,
+):
+    n = lax.axis_size("expert")
+    exp_dev, rank, depth = down_adapter_hidden.shape
+    layer_width = down_adapter_output.shape[2]
+    blocks, _, slots, hidden_width = hidden.shape[1:]
+    tokens = expert_choice_index.shape[0]
+    fits = (
+        lax.axis_size("dp") == 2 and n % 2 == 0 and exp_dev == 2 and rank == 32
+        and tokens == 128 and depth % 128 == 0 and layer_width % 512 == 0
+    )
+    if not fits:
+        return on_device_collectives(
+            hidden, expert_choice_index, gates, down_adapter_hidden, hidden_tangent,
+            down_adapter_output, output_tangent_factor,
+        )
+    experts = exp_dev * n
+    wide = layer_width // 4
+    padded = -(-slots // 16) * 16
+    half = blocks // 2
+    all_rows = experts * 2 * rank
+    own_adapters = jnp.concatenate([down_adapter_hidden, hidden_tangent], axis=1)
+    own_factors = jnp.concatenate([output_tangent_factor, down_adapter_output], axis=1)
+    position, weight = routing_tables(expert_choice_index, gates, experts)
+    own_table = jnp.concatenate([position, weight], axis=1).T
+    dma = pltpu.SemaphoreType.DMA
+    square = pltpu.VMEM((4 * rank, all_rows), F32)
+    grad_a, grad_b = pl.pallas_call(
+        functools.partial(fused_kernel, n, rank, slots),
+        out_shape=(
+            jax.ShapeDtypeStruct((2 * rank, depth), F32),
+            jax.ShapeDtypeStruct((2 * rank, 2 * wide), F32),
+        ),
+        in_specs=[pl.BlockSpec(memory_space=pltpu.VMEM)] * 4,
+        out_specs=[pl.BlockSpec(memory_space=pltpu.VMEM)] * 2,
+        scratch_shapes=[
+            pltpu.VMEM((n, 4 * rank, wide), BF16),
+            pltpu.VMEM((4 * rank, depth), BF16),
+            pltpu.VMEM((n, 2 * experts, tokens), F32),
+            pltpu.VMEM((blocks, padded, 4 * rank), F32),
+            pltpu.VMEM((blocks, padded, 4 * rank), BF16),
+            pltpu.VMEM((n, half, padded, 4 * rank), BF16),
+            pltpu.VMEM((all_rows, half * tokens), BF16),
+            pltpu.VMEM((all_rows, half * tokens), BF16),
+        ] + [square] * 8 + [
+            pltpu.VMEM((2, 4 * rank, half * tokens), BF16),
+            pltpu.VMEM((2, 2 * rank, depth), F32),
+            pltpu.VMEM((2 * rank, depth), F32),
+            pltpu.VMEM((4 * rank, wide), F32),
+            pltpu.VMEM((2 * rank, wide), F32),
+            dma((n,)), dma((n,)), dma((n,)), dma((n,)), dma((n,)), dma((n,)),
+            dma((8,)), dma((8,)), dma((3,)),
+        ],
+        compiler_params=pltpu.CompilerParams(
+            collective_id=0, has_side_effects=True, vmem_limit_bytes=48 * 1024 * 1024
+        ),
+    )(
+        hidden[0],
+        own_factors.reshape(4 * rank, layer_width),
+        own_adapters.reshape(4 * rank, depth),
+        own_table,
+    )
+    return grad_a.reshape(2, rank, depth), grad_b.reshape(2, rank, 2 * wide)
+
+
 def solution(mesh):
     placed = (
         P(("dom", "dp"), None, "expert", None, None),

time: 142 us -> 95.4 us (0.67)
  Pallas kernels: 0 us -> 87 us
  waiting for transfers between devices: 64.5 us -> 0 us
  blocking collectives: 37.8 us -> 0 us
  matrix products: 18.9 us -> 0.2 us
  between operations: 14 us -> 0.67 us
    pallas_call x0 -> x1, Pallas kernels: none -> 87 us  [on_device(): pl.pallas_call(functools.partial(fused_kernel, n, rank, slots), out_shape...]
    all_gather x2 -> x0, waiting for transfers between devices: 50.6 us -> none  [the longest x1 38.5 us: on_device(): factors = lax.all_gather(stacked_share, 'expert', axis=0, tiled=True)]
    all_gather x2 -> x0, blocking collectives: 22.5 us -> none  [the longest x1 14.7 us: on_device(): lax.all_gather(jnp.concatenate([position, weight], axis=1), 'expert', axi...]
    dot_general x8 -> x0, matrix products: 18.7 us -> none  [the longest x1 3.25 us: on_device(): jnp.einsum('rm,eam->rea', factors, own_output, preferred_element_type=F32)]
    psum x1 -> x0, blocking collectives: 15.2 us -> none  [on_device(): gram, mixing = lax.psum((gram, mixing), 'dp')]
    reduce_scatter x1 -> x0, waiting for transfers between devices: 10.4 us -> none  [on_device(): grad_a = lax.psum_scatter(part_a, 'dp', scatter_dimension=2, tiled=True)]
    psum x1 -> x0, waiting for transfers between devices: 3.33 us -> none  [on_device(): gram, mixing = lax.psum((gram, mixing), 'dp')]
    unnamed x15 -> x3, local copies, waits for them, and re-layouts: 0.27 us -> 3.59 us
  transfers between devices with their start and end apart: 4 -> 0, of which waited for: 4 -> 0; matrix products, arithmetic and copies ran while one was open for 16% -> 0% of each run, Pallas kernels for 0% -> 0%
where the time goes in v2:
time: 95.4 us; the launch traced here: 95.1 us
  Pallas kernels  87 us (91%)
  other arithmetic  3.62 us (4%)
  local copies, waits for them, and re-layouts  3.59 us (4%)
    pallas_call x1, Pallas kernels, on_device(): pl.pallas_call(functools.partial(fused_kernel, n, rank, slots), out_shape...  87 us
    unnamed x3, local copies, waits for them, and re-layouts  3.59 us

profile of v2, /device:TPU:0, one launch (start us, length us, event | category | flops | bytes accessed | tf_op | source)
XLA Modules:
  0.0 95.1 jit_solution(15391877846611462485)
XLA Ops:
  0.6 0.7 fusion
  1.3 0.2 convolution_select_fusion
  1.5 0.7 select_reduce_fusion
  2.3 0.9 pad_maximum_fusion.1
  3.2 1.2 %pad_maximum_fusion = bf16[2,64,3584]{2,1,0:T(8,128)(2,1)S(1)} fusion(bf16[2,32,3584]{2,1,0:T(8,128)(2,1)} %param.12, bf16[2,32,3584]{2,1,0:T(8,128)(2,1)} %param.13), kind=kLoop, calls=%fused_computation.2 | loop fusion | flops 1835008 | bytes 1835008 | tf_op jit(solution)/shard_map/concatenate | solution.py:376
  4.5 2.2 %copy.14 = bf16[1,8,2,66,1280]{4,3,2,1,0:T(8,128)(2,1)S(1)} copy(bf16[1,8,2,66,1280]{4,2,3,1,0:T(2,128)(2,1)} %param.7) | data formatting | bytes 5406720 | tf_op args[0]
  6.6 87.0 %shard_map.86 = (f32[64,640]{1,0:T(8,128)S(1)}, f32[64,1792]{1,0:T(8,128)S(1)}) custom-call(bf16[8,2,66,1280]{3,2,1,0:T(8,128)(2,1)S(1)} %bitcast.10, bf16[128,3584]{1,0:T(8,128)(2,1)S(1)} %bitcast.11, bf16[128,640]{1,0:T(8,128)(2,1)S(1)} %bitcast.12, f32[32,128]{1,0:T(8,128)S(1)} %maximum_bitcast_fusion.own_table), custom_call_target="tpu_custom_call" | custom-call | tf_op jit(solution)/shard_map/pallas_call | solution.py:381
  93.7 0.7 copy.17
  94.3 0.8 copy.18
  (2 shorter events, 0.0 us)

commit v3 on v2

--- a/solution.py
+++ b/solution.py
@@ -111,12 +111,13 @@
     hidden, own_factors, own_adapters, own_table,
     grad_a, grad_b,
     factors, adapters, tables, proj_wide, proj, rows_of,
-    g_high, g_low, mix, mix_core, mix_sum, mix_dp, gram, gram_core, gram_sum, gram_dp,
+    g_high, g_low, mix, mix_core, mix_sum, gram, gram_core, gram_sum, mix_out, mix_dp, gram_out, gram_dp,
     back, pa, pa_in, gb, gb_in,
-    f_send, f_recv, p_send, p_recv, t_send, t_recv, m_send, m_recv, local,
+    f_send, f_recv, p_send, p_recv, t_send, t_recv, h_send, h_recv, m_send, m_recv, local,
 ):
     me = lax.axis_index("expert")
     x = lax.axis_index("dp")
+    y = lax.axis_index("dom")
     core = lax.rem(me, 2)
     chip = me // 2
     blocks = hidden.shape[0]
@@ -137,7 +138,8 @@
             barrier, inc=1, device_id={"expert": lax.rem(me + d, n)}, device_id_type=MESH
         )
     pl.semaphore_signal(barrier, inc=1, device_id={"dp": 1 - x}, device_id_type=MESH)
-    pl.semaphore_wait(barrier, n)
+    pl.semaphore_signal(barrier, inc=1, device_id={"dom": 1 - y}, device_id_type=MESH)
+    pl.semaphore_wait(barrier, n + 1)
 
     def to_dp(k, src, dst):
         return pltpu.make_async_remote_copy(
@@ -162,12 +164,22 @@
 
     adapter_copy = to_dp(0, own_adapters, adapters)
     adapter_copy.start()
-    t_copies, f_copies, p_copies = {}, {}, {}
+    t_copies, f_copies, p_copies, h_copies = {}, {}, {}, {}
     for d in range(1, n):
         t_copies[d] = to_peer(d, own_table, tables.at[me], t_send, t_recv)
         t_copies[d].start()
         c_to = lax.rem(me + d, 2)
-        f_copies[d] = to_peer(d, own_factors.at[:, columns_of(c_to)], factors.at[me], f_send, f_recv)
+        kept = pl.ds(pl.multiple_of(y * rank, rank), 3 * rank)
+        f_copies[d] = to_peer(
+            d, own_factors.at[kept, columns_of(c_to)], factors.at[me, kept], f_send, f_recv
+        )
+        given = pl.ds(pl.multiple_of(y * 3 * rank, rank), rank)
+        source = lax.rem(me + n - d, n)
+        h_copies[d] = pltpu.make_async_remote_copy(
+            src_ref=factors.at[source, given], dst_ref=factors.at[source, given],
+            send_sem=h_send.at[d], recv_sem=h_recv.at[d],
+            device_id={"dom": 1 - y}, device_id_type=MESH,
+        )
         p_copies[d] = to_peer(d, proj.at[pl.ds(half * c_to, half)], rows_of.at[me], p_send, p_recv)
     order = [d for k in range(1, n // 2 + 1) for d in sorted({k, n - k})]
     early = order[: max(1, n // 2 - 1)]
@@ -230,17 +242,25 @@
                 g_high[where, t * tokens:(t + 1) * tokens] = high
                 g_low[where, t * tokens:(t + 1) * tokens] = (piece - high.astype(F32)).astype(BF16)
 
-    def chip_rows(ref, offset):
+    def chip_rows(ref):
         return jnp.concatenate(
             [
-                ref[pl.ds(pl.multiple_of(chip * 4 * two + i * two + offset, rank), rank), :]
-                for i in range(4)
+                ref[pl.ds(pl.multiple_of(chip * 4 * two + first, rank), rank), :]
+                for first in (rank, two, pair + rank, pair + two)
             ],
             axis=0,
         )
 
-    a_high = chip_rows(g_high, 0)
-    a_low = chip_rows(g_low, 0)
+    core_rows = pl.ds(pl.multiple_of(core * two, two), two)
+
+    def hand_over(d):
+        f_copies[d].wait_recv()
+        h_copies[d].start()
+
+    for d in early:
+        hand_over(d)
+    a_high = chip_rows(g_high)
+    a_low = chip_rows(g_low)
     a_both = jnp.concatenate([a_high, a_low], axis=0)
     tile = 2 * pair
     for r in range(0, experts * two, tile):
@@ -251,40 +271,52 @@
     mix_copy.start()
     mix_copy.wait_recv()
     mix_sum[...] = mix[...] + mix_core[...]
-    mix_dp_copy = to_dp(2, mix_sum, mix_dp)
+    mix_out[...] = mix_sum[core_rows, :].astype(BF16)
+    mix_dp_copy = to_dp(2, mix_out, mix_dp.at[core])
     mix_dp_copy.start()
+    for d in late:
+        hand_over(d)
+    mix_dp_copy.wait_recv()
+    mix_share = to_core(8, mix_dp.at[core], mix_dp.at[core])
+    mix_share.start()
+
+    def both_cores(ref):
+        return jnp.concatenate([ref[0], ref[1]], axis=0).astype(F32)
 
     f_local.wait()
-    sibling = me + 1 - 2 * core
-    waited = set()
-    f_copies[1].wait_recv()
-    f_copies[n - 1].wait_recv()
+    h_copies[1].wait_recv()
+    h_copies[n - 1].wait_recv()
     waited = {0, 1, n - 1}
     outs = jnp.concatenate(
         [
-            factors[2 * chip + i, j * two + rank:(j + 1) * two, :]
+            factors[2 * chip + i, first:first + rank, :]
             for i in range(2)
-            for j in range(2)
+            for first in (0, 3 * rank)
         ],
         axis=0,
     )
     for d in [0] + order:
         if d not in waited:
-            f_copies[d].wait_recv()
+            h_copies[d].wait_recv()
         q = lax.rem(me + n - d, n)
         gram[:, pl.ds(pl.multiple_of(q * pair, pair), pair)] = dot(outs, factors[q], NT)
     gram_copy = to_core(3, gram, gram_core)
     gram_copy.start()
     gram_copy.wait_recv()
     gram_sum[...] = gram[...] + gram_core[...]
-    gram_dp_copy = to_dp(4, gram_sum, gram_dp)
+    gram_out[...] = gram_sum[core_rows, :].astype(BF16)
+    gram_dp_copy = to_dp(4, gram_out, gram_dp.at[core])
     gram_dp_copy.start()
 
-    mix_dp_copy.wait_recv()
-    m_high, m_low = split_two(mix_sum[...] + mix_dp[...])
+    mix_share.wait_recv()
+    m_high, m_low = split_two(mix_sum[...] + both_cores(mix_dp))
     m_both = jnp.concatenate([m_high, m_low], axis=0)
     total = None
     for q in range(n):
+        if q == n // 2:
+            gram_dp_copy.wait_recv()
+            gram_share = to_core(9, gram_dp.at[core], gram_dp.at[core])
+            gram_share.start()
         term = dot(m_both[:, q * pair:(q + 1) * pair], factors[q])
         total = term if total is None else total + term
     gb[...] = total[:quad] + total[quad:]
@@ -294,8 +326,8 @@
     other = pl.ds(pl.multiple_of((1 - core) * wide, 128), wide)
     grad_b[:, mine] = gb[pl.ds(pl.multiple_of(core * two, two), two), :]
 
-    gram_dp_copy.wait_recv()
-    k_high, k_low = split_two(gram_sum[...] + gram_dp[...])
+    gram_share.wait_recv()
+    k_high, k_low = split_two(gram_sum[...] + both_cores(gram_dp))
     k_both = jnp.concatenate([k_high, k_low], axis=0)
     for t in range(half):
         cols = slice(t * tokens, (t + 1) * tokens)
@@ -338,7 +370,9 @@
         t_copies[d].wait_send()
         f_copies[d].wait_send()
         p_copies[d].wait_send()
+        h_copies[d].wait_send()
     for copy in (
+        mix_share, gram_share,
         adapter_copy, mix_copy, mix_dp_copy, gram_copy, gram_dp_copy, gb_copy, back_copy, pa_copy
     ):
         copy.wait_send()
@@ -359,7 +393,7 @@
     blocks, _, slots, hidden_width = hidden.shape[1:]
     tokens = expert_choice_index.shape[0]
     fits = (
-        lax.axis_size("dp") == 2 and n % 2 == 0 and exp_dev == 2 and rank == 32
+        lax.axis_size("dp") == 2 and lax.axis_size("dom") == 2 and n % 2 == 0 and exp_dev == 2 and rank == 32
         and tokens == 128 and depth % 128 == 0 and layer_width % 512 == 0
     )
     if not fits:
@@ -372,11 +406,20 @@
     padded = -(-slots // 16) * 16
     half = blocks // 2
     all_rows = experts * 2 * rank
-    own_adapters = jnp.concatenate([down_adapter_hidden, hidden_tangent], axis=1)
-    own_factors = jnp.concatenate([output_tangent_factor, down_adapter_output], axis=1)
+    own_adapters = jnp.concatenate(
+        [hidden_tangent[0], down_adapter_hidden[0], down_adapter_hidden[1], hidden_tangent[1]]
+    )
+    own_factors = jnp.concatenate(
+        [
+            down_adapter_output[0], output_tangent_factor[0],
+            output_tangent_factor[1], down_adapter_output[1],
+        ]
+    )
     position, weight = routing_tables(expert_choice_index, gates, experts)
     own_table = jnp.concatenate([position, weight], axis=1).T
     dma = pltpu.SemaphoreType.DMA
+    narrow = pltpu.VMEM((2 * rank, all_rows), BF16)
+    paired = pltpu.VMEM((2, 2 * rank, all_rows), BF16)
     square = pltpu.VMEM((4 * rank, all_rows), F32)
     grad_a, grad_b = pl.pallas_call(
         functools.partial(fused_kernel, n, rank, slots),
@@ -395,22 +438,22 @@
             pltpu.VMEM((n, half, padded, 4 * rank), BF16),
             pltpu.VMEM((all_rows, half * tokens), BF16),
             pltpu.VMEM((all_rows, half * tokens), BF16),
-        ] + [square] * 8 + [
+        ] + [square] * 6 + [narrow, paired, narrow, paired] + [
             pltpu.VMEM((2, 4 * rank, half * tokens), BF16),
             pltpu.VMEM((2, 2 * rank, depth), F32),
             pltpu.VMEM((2 * rank, depth), F32),
             pltpu.VMEM((4 * rank, wide), F32),
             pltpu.VMEM((2 * rank, wide), F32),
-            dma((n,)), dma((n,)), dma((n,)), dma((n,)), dma((n,)), dma((n,)),
-            dma((8,)), dma((8,)), dma((3,)),
+            dma((n,)), dma((n,)), dma((n,)), dma((n,)), dma((n,)), dma((n,)), dma((n,)), dma((n,)),
+            dma((10,)), dma((10,)), dma((3,)),
         ],
         compiler_params=pltpu.CompilerParams(
             collective_id=0, has_side_effects=True, vmem_limit_bytes=48 * 1024 * 1024
         ),
     )(
         hidden[0],
-        own_factors.reshape(4 * rank, layer_width),
-        own_adapters.reshape(4 * rank, depth),
+        own_factors,
+        own_adapters,
         own_table,
     )
     return grad_a.reshape(2, rank, depth), grad_b.reshape(2, rank, 2 * wide)

time: 95.4 us -> 82.3 us (0.86)
  Pallas kernels: 87 us -> 74.9 us
  other arithmetic: 3.62 us -> 1.53 us
  local copies, waits for them, and re-layouts: 3.59 us -> 4.76 us
    pallas_call x1, Pallas kernels: 87 us -> 74.9 us  [on_device(): pl.pallas_call(functools.partial(fused_kernel, n, rank, slots), out_shape...]
    squeeze x0 -> x2, local copies, waits for them, and re-layouts: none -> 2.34 us  [the longest x1 1.48 us: on_device(): output_tangent_factor[0]]
    concatenate x2, other arithmetic: 2.17 us -> 0.08 us  [the longest x1 0.06 us: on_device(): jnp.concatenate([down_adapter_output[0], output_tangent_factor[0], output...]
    unnamed x3 -> x5, local copies, waits for them, and re-layouts: 3.59 us -> 2.42 us
where the time goes in v3:
time: 82.3 us; the launch traced here: 82.1 us
  Pallas kernels  74.9 us (91%)
  local copies, waits for them, and re-layouts  4.76 us (6%)
  other arithmetic  1.53 us (2%)
    pallas_call x1, Pallas kernels, on_device(): pl.pallas_call(functools.partial(fused_kernel, n, rank, slots), out_shape...  74.9 us
    unnamed x5, local copies, waits for them, and re-layouts  2.42 us

profile of v3, /device:TPU:0, one launch (start us, length us, event | category | flops | bytes accessed | tf_op | source)
XLA Modules:
  0.0 82.1 jit_solution(2879579834459209400)
XLA Ops:
  0.6 0.7 fusion
  1.3 0.2 convolution_select_fusion
  1.5 0.7 select_reduce_fusion
  2.3 0.9 %slice_bitcast_fusion.6 = (bf16[32,640]{1,0:T(8,128)(2,1)S(1)}, bf16[32,640]{1,0:T(8,128)(2,1)S(1)}, bf16[32,640]{1,0:T(8,128)(2,1)S(1)}, bf16[32,640]{1,0:T(8,128)(2,1)S(1)}) fusion(bf16[2,32,640]{2,1,0:T(8,128)(2,1)} %param.10, bf16[2,32,640]{2,1,0:T(8,128)(2,1)} %param.11), kind=kLoop, calls=%fused_computation.15 | loop fusion | bytes 327680 | tf_op jit(solution)/shard_map/squeeze | solution.py:410
  3.2 0.0 copy-start
  3.2 1.5 %slice_bitcast_fusion.2 = (bf16[32,3584]{1,0:T(8,128)(2,1)S(1)}, bf16[32,3584]{1,0:T(8,128)(2,1)S(1)}, bf16[32,3584]{1,0:T(8,128)(2,1)S(1)}, bf16[32,3584]{1,0:T(8,128)(2,1)S(1)}) fusion(bf16[2,32,3584]{2,1,0:T(8,128)(2,1)} %param.13, bf16[2,32,3584]{2,1,0:T(8,128)(2,1)} %param.12), kind=kLoop, calls=%fused_computation.5 | loop fusion | bytes 1835008 | tf_op jit(solution)/shard_map/squeeze | solution.py:414
  4.7 0.1 pad_maximum_fusion.own_factors
  4.8 0.6 copy-done
  5.3 0.4 copy.14
  5.7 74.9 %shard_map.86 = (f32[64,640]{1,0:T(8,128)S(1)}, f32[64,1792]{1,0:T(8,128)S(1)}) custom-call(bf16[8,2,66,1280]{3,2,1,0:T(8,128)(2,1)S(1)} %bitcast.24, bf16[128,3584]{1,0:T(8,128)(2,1)S(1)} %pad_maximum_fusion.own_factors, bf16[128,640]{1,0:T(8,128)(2,1)S(1)} %pad_maximum_fusion.1.own_adapters, f32[32,128]{1,0:T(8,128)S(1)} %maximum_bitcast_fusion.own_table), custom_call_target="tpu_custom_call" | custom-call | tf_op jit(solution)/shard_map/pallas_call | solution.py:424
  80.6 0.7 copy.17
  81.3 0.8 copy.18
  (3 shorter events, 0.0 us)
Async XLA Ops:
  3.2 2.2 %copy-start = (bf16[1,8,2,66,1280]{4,2,3,1,0:T(2,128)(2,1)S(1)}, bf16[1,8,2,66,1280]{4,2,3,1,0:T(2,128)(2,1)}, u32[]{:S(2)}) copy-start(bf16[1,8,2,66,1280]{4,2,3,1,0:T(2,128)(2,1)} %param.7) | copy-start | bytes 8110084

commit v4 on v3

--- a/solution.py
+++ b/solution.py
@@ -112,7 +112,7 @@
     grad_a, grad_b,
     factors, adapters, tables, proj_wide, proj, rows_of,
     g_high, g_low, mix, mix_core, mix_sum, gram, gram_core, gram_sum, mix_out, mix_dp, gram_out, gram_dp,
-    back, pa, pa_in, gb, gb_in,
+    back, pa, pa_out, pa_in, gb, gb_in,
     f_send, f_recv, p_send, p_recv, t_send, t_recv, h_send, h_recv, m_send, m_recv, local,
 ):
     me = lax.axis_index("expert")
@@ -359,12 +359,13 @@
             acc = term if acc is None else acc + term
         for h in range(2):
             pa[h, j * rank:(j + 1) * rank, :] = acc[:, h * depth:(h + 1) * depth]
-    pa_copy = to_dp(7, pa.at[1 - x], pa_in)
+    pa_out[...] = pa[1 - x].astype(BF16)
+    pa_copy = to_dp(7, pa_out, pa_in)
     pa_copy.start()
     gb_copy.wait_recv()
     grad_b[:, other] = gb_in[...]
     pa_copy.wait_recv()
-    grad_a[...] = pa[x] + pa_in[...]
+    grad_a[...] = pa[x] + pa_in[...].astype(F32)
 
     for d in range(1, n):
         t_copies[d].wait_send()
@@ -441,7 +442,8 @@
         ] + [square] * 6 + [narrow, paired, narrow, paired] + [
             pltpu.VMEM((2, 4 * rank, half * tokens), BF16),
             pltpu.VMEM((2, 2 * rank, depth), F32),
-            pltpu.VMEM((2 * rank, depth), F32),
+            pltpu.VMEM((2 * rank, depth), BF16),
+            pltpu.VMEM((2 * rank, depth), BF16),
             pltpu.VMEM((4 * rank, wide), F32),
             pltpu.VMEM((2 * rank, wide), F32),
             dma((n,)), dma((n,)), dma((n,)), dma((n,)), dma((n,)), dma((n,)), dma((n,)), dma((n,)),

time: 82.3 us -> 80.6 us (0.979)
  Pallas kernels: 74.9 us -> 73.2 us
    pallas_call x1, Pallas kernels: 74.9 us -> 73.2 us  [on_device(): pl.pallas_call(functools.partial(fused_kernel, n, rank, slots), out_shape...]
where the time goes in v4:
time: 80.6 us; the launch traced here: 80.3 us
  Pallas kernels  73.2 us (91%)
  local copies, waits for them, and re-layouts  4.76 us (6%)
  other arithmetic  1.53 us (2%)
    pallas_call x1, Pallas kernels, on_device(): pl.pallas_call(functools.partial(fused_kernel, n, rank, slots), out_shape...  73.2 us
    unnamed x5, local copies, waits for them, and re-layouts  2.42 us

profile of v4, /device:TPU:0, one launch (start us, length us, event | category | flops | bytes accessed | tf_op | source)
XLA Modules:
  0.0 80.3 jit_solution(10069524015405162622)
XLA Ops:
  0.6 0.7 fusion
  1.3 0.2 convolution_select_fusion
  1.5 0.7 select_reduce_fusion
  2.3 0.9 %slice_bitcast_fusion.6 = (bf16[32,640]{1,0:T(8,128)(2,1)S(1)}, bf16[32,640]{1,0:T(8,128)(2,1)S(1)}, bf16[32,640]{1,0:T(8,128)(2,1)S(1)}, bf16[32,640]{1,0:T(8,128)(2,1)S(1)}) fusion(bf16[2,32,640]{2,1,0:T(8,128)(2,1)} %param.10, bf16[2,32,640]{2,1,0:T(8,128)(2,1)} %param.11), kind=kLoop, calls=%fused_computation.15 | loop fusion | bytes 327680 | tf_op jit(solution)/shard_map/squeeze | solution.py:411
  3.2 0.0 copy-start
  3.2 1.5 %slice_bitcast_fusion.2 = (bf16[32,3584]{1,0:T(8,128)(2,1)S(1)}, bf16[32,3584]{1,0:T(8,128)(2,1)S(1)}, bf16[32,3584]{1,0:T(8,128)(2,1)S(1)}, bf16[32,3584]{1,0:T(8,128)(2,1)S(1)}) fusion(bf16[2,32,3584]{2,1,0:T(8,128)(2,1)} %param.13, bf16[2,32,3584]{2,1,0:T(8,128)(2,1)} %param.12), kind=kLoop, calls=%fused_computation.5 | loop fusion | bytes 1835008 | tf_op jit(solution)/shard_map/squeeze | solution.py:415
  4.7 0.1 pad_maximum_fusion.own_factors
  4.8 0.6 copy-done
  5.3 0.4 copy.14
  5.7 73.2 %shard_map.86 = (f32[64,640]{1,0:T(8,128)S(1)}, f32[64,1792]{1,0:T(8,128)S(1)}) custom-call(bf16[8,2,66,1280]{3,2,1,0:T(8,128)(2,1)S(1)} %bitcast.24, bf16[128,3584]{1,0:T(8,128)(2,1)S(1)} %pad_maximum_fusion.own_factors, bf16[128,640]{1,0:T(8,128)(2,1)S(1)} %pad_maximum_fusion.1.own_adapters, f32[32,128]{1,0:T(8,128)S(1)} %maximum_bitcast_fusion.own_table), custom_call_target="tpu_custom_call" | custom-call | tf_op jit(solution)/shard_map/pallas_call | solution.py:425
  78.9 0.7 copy.17
  79.6 0.8 copy.18
  (3 shorter events, 0.0 us)
Async XLA Ops:
  3.2 2.2 %copy-start = (bf16[1,8,2,66,1280]{4,2,3,1,0:T(2,128)(2,1)S(1)}, bf16[1,8,2,66,1280]{4,2,3,1,0:T(2,128)(2,1)}, u32[]{:S(2)}) copy-start(bf16[1,8,2,66,1280]{4,2,3,1,0:T(2,128)(2,1)} %param.7) | copy-start | bytes 8110084
